TPU v7x, 128 devices: a whole 4x4x4 slice. The times are simulated.
128 devices in a mesh: sib: 2 (over x_lo), row: 8 (over y, core), col: 8 (over z, x_hi).
Axes of the slice: x: 4 (x_hi: 2, x_lo: 2; x = x_hi * 2 + x_lo), y: 4, z: 4, core: 2. Of those that a mesh axis runs over, the one named last changes fastest.
Arguments:
- child_tiles: float32 [2, 64, 128, 128, 128], P('sib', ('row', 'col')), may hold values from -6 to 6
- child_rows: int32 [2, 64], P('sib'), may hold values from 0 to 127, as said below
- child_slots: int32 [2, 64, 128], P('sib', ('row', 'col')), may hold values from 0 to 4095, as said below
- tile_count: int32 [2, 64], P('sib', ('row', 'col')), may hold values from 64 to 128, as said below
- inverses: float32 [2, 512, 512], replicated, as said below
Outputs:
- factored: float32 [8, 16, 16, 8, 128, 128], P(None, ('sib', 'row'), None, 'col')
Inputs may be any that keep to these rules, and one draw needn't show every extreme that they name: `child_rows`: A child's entries are distinct; entry i leaves the same remainder as i when divided by the number of grid rows of the parent. `child_slots`: call the owner of parent tile (I, J) the grid row I mod (number of grid rows) and grid column J mod (number of grid columns). Among the live slots of one device at most 2 carry tiles with one owner; in every draw some device reaches 2 for some owner. `tile_count`: some device of each child has all 128 slots live. `inverses`: each matrix is lower triangular with positive diagonal.
All inputs are finite; a program needn't handle non-finite values.
Results may differ from a plain program's by a relative error of at most 0.00012.
Values sent between devices are 32-bit elements; how exact they have to be, the bound alone decides.
No kernel may reach another device: no remote copies, remote signals or barrier semaphores. Data moves between devices by JAX's collectives and lax.ppermute only.
A program may use at most 192 MiB of HBM per device.

v0:
```python
import jax
import jax.numpy as jnp
from jax import lax
from jax.sharding import PartitionSpec as P

NF = 16384
TILE = 128
PANEL = 512
NPANEL = 2
CHILD_TILES = 64
CAP = 2


def broadcast(value, axis, source):
    kept = jnp.where(lax.axis_index(axis) == source, value, 0).astype(value.dtype)
    return lax.psum(kept, axis)


def local(child_tiles, child_rows, child_slots, tile_count, inverses):
    grid_rows = lax.axis_size("sib") * lax.axis_size("row")
    columns = lax.axis_size("col")
    devices = grid_rows * columns
    tile_order = NF // TILE
    local_rows = tile_order // grid_rows
    local_cols = tile_order // columns
    tile_data = child_tiles[0, 0]
    slot_ids = child_slots[0, 0]
    live_count = tile_count[0, 0]
    row_list = child_rows[0]
    slot_total = slot_ids.shape[0]
    child_row = slot_ids // CHILD_TILES
    child_col = slot_ids % CHILD_TILES
    positions = jnp.arange(CHILD_TILES, dtype=jnp.int32)
    parent_row = jnp.sum(
        jnp.where(child_row[:, None] == positions[None, :], row_list[None, :], 0), axis=1
    )
    parent_col = jnp.sum(
        jnp.where(child_col[:, None] == positions[None, :], row_list[None, :], 0), axis=1
    )
    owner_index = parent_row % grid_rows * columns + parent_col % columns
    target = parent_row // grid_rows * local_cols + parent_col // columns
    slot_order = jnp.arange(slot_total, dtype=jnp.int32)
    is_live = slot_order < live_count
    earlier = (
        (owner_index[:, None] == owner_index[None, :])
        & is_live[None, :]
        & (slot_order[None, :] < slot_order[:, None])
    )
    slot_rank = jnp.sum(earlier.astype(jnp.int32), axis=1)
    slot_place = jnp.where(is_live, owner_index * CAP + slot_rank, devices * CAP)
    outgoing = (
        jnp.zeros((devices * CAP, TILE, TILE), jnp.float32)
        .at[slot_place]
        .set(tile_data, mode="drop")
    )
    destined = jnp.zeros((devices * CAP,), jnp.int32).at[slot_place].set(target, mode="drop")
    arrived, landing = (
        lax.all_to_all(
            outgoing.reshape(devices, CAP, TILE, TILE),
            ("sib", "row", "col"),
            split_axis=0,
            concat_axis=0,
            tiled=True,
        ),
        lax.all_to_all(
            destined.reshape(devices, CAP),
            ("sib", "row", "col"),
            split_axis=0,
            concat_axis=0,
            tiled=True,
        ),
    )
    front_tiles = jnp.zeros((local_rows * local_cols, TILE, TILE), jnp.float32)
    front_tiles = front_tiles.at[landing.reshape(-1)].add(arrived.reshape(-1, TILE, TILE))
    front_tiles = front_tiles.reshape(local_rows, local_cols, TILE, TILE)
    my_row = lax.axis_index(("sib", "row"))
    my_col = lax.axis_index("col")
    panel_tiles = PANEL // TILE
    root_count = grid_rows // columns
    tile_ids = jnp.arange(local_rows, dtype=jnp.int32) * grid_rows + my_row
    for panel_step in range(NPANEL):
        first_tile = panel_tiles * panel_step
        below_tile = first_tile + panel_tiles
        column_slot = first_tile // columns
        start_col = first_tile % columns
        is_below = tile_ids >= below_tile
        weights = inverses[panel_step]
        column_block = front_tiles[:, column_slot]
        holds_panel = (my_col >= start_col) & (my_col < start_col + panel_tiles)
        offset = jnp.clip(my_col - start_col, 0, panel_tiles - 1)
        everyone = lax.all_gather(column_block[None], "col", axis=0, tiled=True)
        chosen = everyone[start_col : start_col + panel_tiles]
        panel_rows = chosen.transpose(1, 2, 0, 3).reshape(local_rows * TILE, PANEL)
        factor = jnp.dot(panel_rows, weights.T, precision=lax.Precision.HIGHEST)
        factor = (
            factor.reshape(local_rows, TILE, PANEL) * is_below.astype(jnp.float32)[:, None, None]
        )
        panel_piece = lax.dynamic_slice_in_dim(factor, offset * TILE, TILE, 2)
        replace = is_below[:, None, None] & holds_panel
        front_tiles = front_tiles.at[:, column_slot].set(
            jnp.where(replace, panel_piece, column_block)
        )
        received = [
            broadcast(factor, ("sib", "row"), root_step * columns + my_col)
            for root_step in range(root_count)
        ]
        column_factor = jnp.stack(received, 1).reshape(local_cols, TILE, PANEL)
        front_tiles = front_tiles - jnp.einsum(
            "aip,bjp->abij", factor, column_factor, precision=lax.Precision.HIGHEST
        )
    return front_tiles.reshape(local_rows, 1, local_cols, 1, TILE, TILE)


def solution(mesh):
    return jax.shard_map(
        local,
        mesh=mesh,
        in_specs=(
            P("sib", ("row", "col"), None, None, None),
            P("sib", None),
            P("sib", ("row", "col"), None),
            P("sib", ("row", "col")),
            P(),
        ),
        out_specs=P(None, ("sib", "row"), None, "col", None, None),
        check_vma=False,
    )
```

profile of v0, /device:TPU:0, one launch (start us, length us, event | category | flops | bytes accessed | tf_op | source)
XLA Modules:
  0.0 837.8 jit_solution(17602744139437200190)
XLA Ops:
  10.6 11.1 %all-to-all-start = ((s32[128,1,2]{2,1,0:T(1,128)}), s32[128,1,2]{2,1,0:T(1,128)S(1)}, u32[]{:S(2)}, u32[]{:S(2)}) async-start(s32[128,1,2]{2,1,0:T(1,128)} %bitcast.7), calls=%async_computation | async-start | bytes 131072 | tf_op jit(solution)/shard_map/all_to_all | solution.py:65
  21.7 7.9 broadcast_in_dim.69
  29.6 23.2 %scatter_fusion = f32[256,128,128]{2,1,0:T(8,128)} fusion(f32[256,128,128]{2,1,0:T(8,128)} %broadcast_in_dim.69, s32[128]{0:T(128)S(1)} %fusion.16, f32[128,128,128]{2,1,0:T(8,128)} %bitcast.120), kind=kCustom, calls=%fused_computation.1 | custom fusion | bytes 25166336 | tf_op jit(solution)/shard_map/scatter | solution.py:54
  52.8 10.2 %all-to-all-start.1 = ((f32[128,2,128,128]{3,2,1,0:T(8,128)}), f32[128,2,128,128]{3,2,1,0:T(8,128)}, u32[]{:S(2)}, u32[]{:S(2)}) async-start(f32[128,2,128,128]{3,2,1,0:T(8,128)} %bitcast.117), calls=%async_computation.1 | async-start | bytes 33554432 | tf_op jit(solution)/shard_map/all_to_all | solution.py:58
  64.6 222.0 %all-to-all-done.1 = f32[128,2,128,128]{3,2,1,0:T(8,128)} async-done(((f32[128,2,128,128]{3,2,1,0:T(8,128)}), f32[128,2,128,128]{3,2,1,0:T(8,128)}, u32[]{:S(2)}, u32[]{:S(2)}) %all-to-all-start.1) | async-done | bytes 16777248 | tf_op jit(solution)/shard_map/all_to_all | solution.py:58
  286.6 4.5 broadcast_in_dim.64
  291.0 51.2 %scatter_fusion.1 = f32[128,128,128]{2,1,0:T(8,128)} fusion(f32[128,128,128]{2,1,0:T(8,128)} %broadcast_in_dim.64, s32[256]{0:T(256)S(1)} %bitcast.125, f32[256,128,128]{2,1,0:T(8,128)} %bitcast.11), kind=kCustom, calls=%fused_computation.2 | custom fusion | flops 4194304 | bytes 50332672 | tf_op jit(solution)/shard_map/scatter-add | solution.py:74
  342.2 1.9 slice_bitcast_fusion.1
  344.3 85.3 %all-gather.5.cloned.1.call-done = f32[64,1,128,128]{3,2,1,0:T(8,128)} async-done(((f32[8,1,128,128]{3,2,1,0:T(8,128)}), f32[64,1,128,128]{3,2,1,0:T(8,128)}) %all-gather.5.cloned.1.call-update) | async-done | bytes 4194320 | tf_op jit(solution)/shard_map/all_gather | solution.py:91
  434.4 5.3 convolution_multiply_fusion.1
  439.7 2.6 select_bitcast_fusion.3
  442.8 7.7 copy.36
  451.4 118.5 %all-reduce.7.cloned.1.call-done = (f32[8,1,128,512]{3,2,0,1:T(8,128)}, f32[8,1,128,512]{3,2,0,1:T(8,128)}) async-done(((f32[8,1,128,512]{3,2,0,1:T(8,128)}, f32[8,1,128,512]{3,2,0,1:T(8,128)}), (f32[8,1,128,512]{3,2,0,1:T(8,128)}, f32[8,1,128,512]{3,2,0,1:T(8,128)})) %all-reduce.7.cloned.1.call-update) | async-done | bytes 4194320 | tf_op jit(solution)/shard_map/psum | solution.py:16
  570.0 2.9 pad_maximum_fusion
  573.5 15.8 %bitcast_subtract_fusion.1 = f32[8,16,128,128]{3,2,0,1:T(8,128)S(1)} fusion(f32[8,16,128,128]{3,2,0,1:T(8,128)} %bitcast_dynamic-update-slice_fusion.1, f32[16,128,512,1]{2,1,3,0:T(8,128)S(1)} %bitcast.118, f32[8,128,512]{2,1,0:T(8,128)S(1)} %convolution_multiply_fusion.1), kind=kOutput, calls=%fused_computation.5 | convolution fusion | flops 12886999040 | bytes 23068672 | tf_op jit(solution)/shard_map/aip,bjp->abij/dot_general | solution.py:108
  589.4 3.4 copy-done
  593.8 72.4 %all-gather.7.cloned.1.call-done = f32[64,1,128,128]{3,2,1,0:T(8,128)} async-done(((f32[8,1,128,128]{3,2,1,0:T(8,128)}), f32[64,1,128,128]{3,2,1,0:T(8,128)}) %all-gather.7.cloned.1.call-update) | async-done | bytes 4194320 | tf_op jit(solution)/shard_map/all_gather | solution.py:91
  669.1 2.0 dot_general.19
  671.1 5.3 convolution_multiply_fusion
  676.4 2.6 select_bitcast_fusion.1
  680.0 126.6 %all-reduce.5.cloned.1.call-done = (f32[8,1,128,512]{3,2,0,1:T(8,128)}, f32[8,1,128,512]{3,2,0,1:T(8,128)}) async-done(((f32[8,1,128,512]{3,2,0,1:T(8,128)}, f32[8,1,128,512]{3,2,0,1:T(8,128)}), (f32[8,1,128,512]{3,2,0,1:T(8,128)}, f32[8,1,128,512]{3,2,0,1:T(8,128)})) %all-reduce.5.cloned.1.call-update) | async-done | bytes 4194320 | tf_op jit(solution)/shard_map/psum | solution.py:16
  806.6 3.1 pad_maximum_fusion.1
  812.0 15.0 %fusion = f32[8,1,16,1,128,128]{5,4,0,2,3,1:T(8,128)S(1)} fusion(f32[8,16,128,128]{3,2,0,1:T(8,128)S(1)} %bitcast.116, f32[16,128,512,1]{2,1,3,0:T(8,128)S(1)} %bitcast.119, f32[8,128,512]{2,1,0:T(8,128)S(1)} %convolution_multiply_fusion), kind=kOutput, calls=%fused_computation.4 | convolution fusion | flops 12886999040 | bytes 23068672 | tf_op jit(solution)/shard_map/aip,bjp->abij/dot_general | solution.py:108
  827.0 4.0 copy.43
  (41 shorter events, 18.9 us)
Async XLA Ops:
  10.6 42.2 %all-to-all-start = ((s32[128,1,2]{2,1,0:T(1,128)}), s32[128,1,2]{2,1,0:T(1,128)S(1)}, u32[]{:S(2)}, u32[]{:S(2)}) async-start(s32[128,1,2]{2,1,0:T(1,128)} %bitcast.7), calls=%async_computation | async-start | bytes 131072 | tf_op jit(solution)/shard_map/all_to_all | solution.py:65
  52.8 233.7 %all-to-all-start.1 = ((f32[128,2,128,128]{3,2,1,0:T(8,128)}), f32[128,2,128,128]{3,2,1,0:T(8,128)}, u32[]{:S(2)}, u32[]{:S(2)}) async-start(f32[128,2,128,128]{3,2,1,0:T(8,128)} %bitcast.117), calls=%async_computation.1 | async-start | bytes 33554432 | tf_op jit(solution)/shard_map/all_to_all | solution.py:58
  63.0 366.5 %all-gather.5.cloned.1.call-start = ((), (), s32[]{:S(2)}) async-start(), calls=%async_computation.2 | async-start | bytes 4718592 | tf_op jit(solution)/shard_map/all_gather | solution.py:91
  344.2 225.8 %all-reduce.7.cloned.1.call-start = ((), (), s32[]{:S(2)}) async-start(), calls=%async_computation.5 | async-start | bytes 8388608 | tf_op jit(solution)/shard_map/psum | solution.py:16
  429.5 1.6 slice-start.2
  442.3 223.9 %all-gather.7.cloned.1.call-start = ((), (), s32[]{:S(2)}) async-start(), calls=%async_computation.3 | async-start | bytes 4718592 | tf_op jit(solution)/shard_map/all_gather | solution.py:91
  589.4 3.4 copy-start
  593.7 212.9 %all-reduce.5.cloned.1.call-start = ((), (), s32[]{:S(2)}) async-start(), calls=%async_computation.4 | async-start | bytes 8388608 | tf_op jit(solution)/shard_map/psum | solution.py:16
  666.1 1.6 slice-start.3
  806.6 3.7 slice-start
  809.7 2.3 slice-start.1
Sparse Core Ops, SparseCore 0:
  344.3 85.1 all-gather.4
  442.4 127.5 all-reduce.6
  593.8 72.2 all-gather.6
  679.2 127.3 all-reduce.4
where the time goes:
time: 847 us; the launch traced here: 838 us
  waiting for transfers between devices  625 us (74%)
  local copies, waits for them, and re-layouts  68.5 us (8%)
  other arithmetic  66.7 us (8%)
  matrix products  41.5 us (5%)
  starting transfers between devices  22 us (3%)
  between operations  14.2 us (2%)
    psum x2, waiting for transfers between devices, broadcast(): return lax.psum(kept, axis)  245 us
    all_to_all x1, waiting for transfers between devices, local(): lax.all_to_all(outgoing.reshape(devices, CAP, TILE, TILE), ('sib', 'row',...  222 us
    all_gather x2, waiting for transfers between devices, local(): everyone = lax.all_gather(column_block[None], 'col', axis=0, tiled=True)  158 us
    scatter-add x1, other arithmetic, local(): front_tiles.at[landing.reshape(-1)].add(arrived.reshape(-1, TILE, TILE))  51.2 us
    dot_general x2, matrix products, local(): jnp.einsum('aip,bjp->abij', factor, column_factor, precision=lax.Precisio...  30.9 us
    scatter x1, local copies, waits for them, and re-layouts, local(): outgoing = jnp.zeros((devices * CAP, TILE, TILE), jnp.float32).at[slot_pl...  23.2 us
  transfers between devices with their start and end apart: 6, of which 5 were waited for; matrix products, arithmetic and copies ran while one was open for 5% of the time, Pallas kernels for 0%

commit v1 on v0

--- a/solution.py
+++ b/solution.py
@@ -9,6 +9,11 @@
 NPANEL = 2
 CHILD_TILES = 64
 CAP = 2
+
+
+def swapped_in(shard, name, dim):
+    outgoing = jnp.stack([shard] * lax.axis_size(name))
+    return jnp.concatenate(lax.all_to_all(outgoing, name, 0, 0), axis=dim)
 
 
 def broadcast(value, axis, source):
@@ -88,7 +93,7 @@
         column_block = front_tiles[:, column_slot]
         holds_panel = (my_col >= start_col) & (my_col < start_col + panel_tiles)
         offset = jnp.clip(my_col - start_col, 0, panel_tiles - 1)
-        everyone = lax.all_gather(column_block[None], "col", axis=0, tiled=True)
+        everyone = swapped_in(column_block[None], "col", 0)
         chosen = everyone[start_col : start_col + panel_tiles]
         panel_rows = chosen.transpose(1, 2, 0, 3).reshape(local_rows * TILE, PANEL)
         factor = jnp.dot(panel_rows, weights.T, precision=lax.Precision.HIGHEST)

time: 847 us -> 807 us (0.953)
  waiting for transfers between devices: 625 us -> 568 us
  starting transfers between devices: 22 us -> 44.6 us
    all_gather x2 -> x0, waiting for transfers between devices: 158 us -> none  [local(): everyone = lax.all_gather(column_block[None], 'col', axis=0, tiled=True)]
    all_to_all x0 -> x2, waiting for transfers between devices: none -> 101 us  [swapped_in(): return jnp.concatenate(lax.all_to_all(outgoing, name, 0, 0), axis=dim)]
    all_to_all x0 -> x2, starting transfers between devices: none -> 22.9 us  [swapped_in(): return jnp.concatenate(lax.all_to_all(outgoing, name, 0, 0), axis=dim)]
    slice x8 -> x0, local copies, waits for them, and re-layouts: 8.72 us -> none  [the longest x6 5.89 us: local(): chosen = everyone[start_col:start_col + panel_tiles]]
where the time goes in v1:
time: 807 us; the launch traced here: 797 us
  waiting for transfers between devices  568 us (70%)
  other arithmetic  66.7 us (8%)
  local copies, waits for them, and re-layouts  61.9 us (8%)
  starting transfers between devices  44.6 us (6%)
  matrix products  42 us (5%)
  between operations  14.5 us (2%)
    psum x2, waiting for transfers between devices, broadcast(): return lax.psum(kept, axis)  244 us
    all_to_all x1, waiting for transfers between devices, local(): lax.all_to_all(outgoing.reshape(devices, CAP, TILE, TILE), ('sib', 'row',...  222 us
    all_to_all x2, waiting for transfers between devices, swapped_in(): return jnp.concatenate(lax.all_to_all(outgoing, name, 0, 0), axis=dim)  101 us
    scatter-add x1, other arithmetic, local(): front_tiles.at[landing.reshape(-1)].add(arrived.reshape(-1, TILE, TILE))  51.2 us
    dot_general x2, matrix products, local(): jnp.einsum('aip,bjp->abij', factor, column_factor, precision=lax.Precisio...  31.3 us
    scatter x1, local copies, waits for them, and re-layouts, local(): outgoing = jnp.zeros((devices * CAP, TILE, TILE), jnp.float32).at[slot_pl...  23.3 us
    all_to_all x2, starting transfers between devices, swapped_in(): return jnp.concatenate(lax.all_to_all(outgoing, name, 0, 0), axis=dim)  22.9 us
  transfers between devices with their start and end apart: 6, of which 5 were waited for; matrix products, arithmetic and copies ran while one was open for 5% of the time, Pallas kernels for 0%

profile of v1, /device:TPU:0, one launch (start us, length us, event | category | flops | bytes accessed | tf_op | source)
XLA Modules:
  0.0 797.3 jit_solution(14512053462493739376)
XLA Ops:
  10.6 11.1 %all-to-all-start = ((s32[128,1,2]{2,1,0:T(1,128)}), s32[128,1,2]{2,1,0:T(1,128)S(1)}, u32[]{:S(2)}, u32[]{:S(2)}) async-start(s32[128,1,2]{2,1,0:T(1,128)} %bitcast.7), calls=%async_computation | async-start | bytes 131072 | tf_op jit(solution)/shard_map/all_to_all | solution.py:70
  21.7 7.8 broadcast_in_dim.69
  29.6 23.3 %scatter_fusion = f32[256,128,128]{2,1,0:T(8,128)} fusion(f32[256,128,128]{2,1,0:T(8,128)} %broadcast_in_dim.69, s32[128]{0:T(128)S(1)} %fusion.28, f32[128,128,128]{2,1,0:T(8,128)} %bitcast.126), kind=kCustom, calls=%fused_computation.1 | custom fusion | bytes 25166336 | tf_op jit(solution)/shard_map/scatter | solution.py:59
  52.8 10.3 %all-to-all-start.1 = ((f32[128,2,128,128]{3,2,1,0:T(8,128)}), f32[128,2,128,128]{3,2,1,0:T(8,128)}, u32[]{:S(2)}, u32[]{:S(2)}) async-start(f32[128,2,128,128]{3,2,1,0:T(8,128)} %bitcast.123), calls=%async_computation.1 | async-start | bytes 33554432 | tf_op jit(solution)/shard_map/all_to_all | solution.py:63
  64.6 222.0 %all-to-all-done.1 = f32[128,2,128,128]{3,2,1,0:T(8,128)} async-done(((f32[128,2,128,128]{3,2,1,0:T(8,128)}), f32[128,2,128,128]{3,2,1,0:T(8,128)}, u32[]{:S(2)}, u32[]{:S(2)}) %all-to-all-start.1) | async-done | bytes 16777248 | tf_op jit(solution)/shard_map/all_to_all | solution.py:63
  286.7 4.5 broadcast_in_dim.64
  291.1 51.2 %scatter_fusion.1 = f32[128,128,128]{2,1,0:T(8,128)} fusion(f32[128,128,128]{2,1,0:T(8,128)} %broadcast_in_dim.64, s32[256]{0:T(256)S(1)} %bitcast.127, f32[256,128,128]{2,1,0:T(8,128)} %bitcast.11), kind=kCustom, calls=%fused_computation.2 | custom fusion | flops 4194304 | bytes 50332672 | tf_op jit(solution)/shard_map/scatter-add | solution.py:79
  345.8 16.3 %all-to-all-start.2 = ((f32[8,1,8,128,128]{4,3,2,1,0:T(8,128)}), f32[8,1,8,128,128]{4,3,2,1,0:T(8,128)}, u32[]{:S(2)}, u32[]{:S(2)}) async-start(f32[8,1,8,128,128]{4,3,2,1,0:T(8,128)} %stack.24), calls=%async_computation.2 | async-start | bytes 8388608 | tf_op jit(solution)/shard_map/all_to_all | solution.py:16
  362.2 51.4 %all-to-all-done.2 = f32[8,1,8,128,128]{4,3,2,1,0:T(8,128)} async-done(((f32[8,1,8,128,128]{4,3,2,1,0:T(8,128)}), f32[8,1,8,128,128]{4,3,2,1,0:T(8,128)}, u32[]{:S(2)}, u32[]{:S(2)}) %all-to-all-start.2) | async-done | bytes 4194336 | tf_op jit(solution)/shard_map/all_to_all | solution.py:16
  413.6 5.3 fusion.9
  418.9 2.6 select_bitcast_fusion.3
  421.6 7.7 copy.29
  430.2 119.7 %all-reduce.7.cloned.1.call-done = (f32[8,1,128,512]{3,2,0,1:T(8,128)}, f32[8,1,128,512]{3,2,0,1:T(8,128)}) async-done(((f32[8,1,128,512]{3,2,0,1:T(8,128)}, f32[8,1,128,512]{3,2,0,1:T(8,128)}), (f32[8,1,128,512]{3,2,0,1:T(8,128)}, f32[8,1,128,512]{3,2,0,1:T(8,128)})) %all-reduce.7.cloned.1.call-update) | async-done | bytes 4194320 | tf_op jit(solution)/shard_map/psum | solution.py:21
  549.9 2.9 pad_maximum_fusion
  553.4 16.3 %bitcast_subtract_fusion.1 = f32[8,16,128,128]{3,2,0,1:T(8,128)S(1)} fusion(f32[8,16,128,128]{3,2,0,1:T(8,128)} %bitcast_dynamic-update-slice_fusion.1, f32[16,128,512,1]{2,1,3,0:T(8,128)S(1)} %bitcast.124, f32[8,128,512]{2,1,0:T(8,128)S(1)} %fusion.9), kind=kOutput, calls=%fused_computation.5 | convolution fusion | flops 12886999040 | bytes 23068672 | tf_op jit(solution)/shard_map/aip,bjp->abij/dot_general | solution.py:113
  569.8 3.4 copy-done
  575.7 6.6 all-to-all-start.3
  582.4 50.0 %all-to-all-done.3 = f32[8,1,8,128,128]{4,3,2,1,0:T(8,128)} async-done(((f32[8,1,8,128,128]{4,3,2,1,0:T(8,128)}), f32[8,1,8,128,128]{4,3,2,1,0:T(8,128)}, u32[]{:S(2)}, u32[]{:S(2)}) %all-to-all-start.3) | async-done | bytes 4194336 | tf_op jit(solution)/shard_map/all_to_all | solution.py:16
  632.5 5.3 fusion.12
  637.8 2.6 select_bitcast_fusion.1
  641.4 124.4 %all-reduce.5.cloned.1.call-done = (f32[8,1,128,512]{3,2,0,1:T(8,128)}, f32[8,1,128,512]{3,2,0,1:T(8,128)}) async-done(((f32[8,1,128,512]{3,2,0,1:T(8,128)}, f32[8,1,128,512]{3,2,0,1:T(8,128)}), (f32[8,1,128,512]{3,2,0,1:T(8,128)}, f32[8,1,128,512]{3,2,0,1:T(8,128)})) %all-reduce.5.cloned.1.call-update) | async-done | bytes 4194320 | tf_op jit(solution)/shard_map/psum | solution.py:21
  765.8 3.1 pad_maximum_fusion.1
  771.2 15.0 %fusion = f32[8,1,16,1,128,128]{5,4,0,2,3,1:T(8,128)S(1)} fusion(f32[8,16,128,128]{3,2,0,1:T(8,128)S(1)} %bitcast.122, f32[16,128,512,1]{2,1,3,0:T(8,128)S(1)} %bitcast.125, f32[8,128,512]{2,1,0:T(8,128)S(1)} %fusion.12), kind=kOutput, calls=%fused_computation.4 | convolution fusion | flops 12886999040 | bytes 23068672 | tf_op jit(solution)/shard_map/aip,bjp->abij/dot_general | solution.py:113
  786.2 4.0 copy.35
  (34 shorter events, 15.9 us)
Async XLA Ops:
  10.6 42.3 %all-to-all-start = ((s32[128,1,2]{2,1,0:T(1,128)}), s32[128,1,2]{2,1,0:T(1,128)S(1)}, u32[]{:S(2)}, u32[]{:S(2)}) async-start(s32[128,1,2]{2,1,0:T(1,128)} %bitcast.7), calls=%async_computation | async-start | bytes 131072 | tf_op jit(solution)/shard_map/all_to_all | solution.py:70
  52.8 233.8 %all-to-all-start.1 = ((f32[128,2,128,128]{3,2,1,0:T(8,128)}), f32[128,2,128,128]{3,2,1,0:T(8,128)}, u32[]{:S(2)}, u32[]{:S(2)}) async-start(f32[128,2,128,128]{3,2,1,0:T(8,128)} %bitcast.123), calls=%async_computation.1 | async-start | bytes 33554432 | tf_op jit(solution)/shard_map/all_to_all | solution.py:63
  345.8 67.8 %all-to-all-start.2 = ((f32[8,1,8,128,128]{4,3,2,1,0:T(8,128)}), f32[8,1,8,128,128]{4,3,2,1,0:T(8,128)}, u32[]{:S(2)}, u32[]{:S(2)}) async-start(f32[8,1,8,128,128]{4,3,2,1,0:T(8,128)} %stack.24), calls=%async_computation.2 | async-start | bytes 8388608 | tf_op jit(solution)/shard_map/all_to_all | solution.py:16
  362.2 187.7 %all-reduce.7.cloned.1.call-start = ((), (), s32[]{:S(2)}) async-start(), calls=%async_computation.5 | async-start | bytes 8388608 | tf_op jit(solution)/shard_map/psum | solution.py:21
  569.7 3.4 copy-start
  575.7 56.8 %all-to-all-start.3 = ((f32[8,1,8,128,128]{4,3,2,1,0:T(8,128)}), f32[8,1,8,128,128]{4,3,2,1,0:T(8,128)}, u32[]{:S(2)}, u32[]{:S(2)}) async-start(f32[8,1,8,128,128]{4,3,2,1,0:T(8,128)} %stack.28), calls=%async_computation.3 | async-start | bytes 8388608 | tf_op jit(solution)/shard_map/all_to_all | solution.py:16
  582.2 183.6 %all-reduce.5.cloned.1.call-start = ((), (), s32[]{:S(2)}) async-start(), calls=%async_computation.4 | async-start | bytes 8388608 | tf_op jit(solution)/shard_map/psum | solution.py:21
  765.8 3.7 slice-start
  768.9 2.3 slice-start.1
Sparse Core Ops, SparseCore 0:
  421.7 128.1 all-reduce.6
  640.6 125.2 all-reduce.4
